TPU v7x, 512 devices: a whole 4x8x8 slice. The times are simulated.
512 devices in a mesh: tm: 128 (over y, z, core), head: 4 (over x).
Axes of the slice: x: 4, y: 8, z: 8, core: 2. Of those that a mesh axis runs over, the one named last changes fastest.
Arguments:
- video_keys: bfloat16 [16384, 4096], P('tm', 'head'), may hold values from -6 to 6
- video_values: bfloat16 [16384, 4096], P('tm', 'head'), may hold values from -12 to 12
- text_queries: bfloat16 [8192, 4096], P('tm', 'head'), may hold values from -64 to 64
- text_keys: bfloat16 [8192, 4096], P('tm', 'head'), may hold values from -7 to 7
- text_values: bfloat16 [8192, 4096], P('tm', 'head'), may hold values from -6 to 6
- boundaries: int32 [128], P('tm'), may hold values from 1 to 16384, as said below
- gate_logit: float32 [32], P('head'), may hold values from -3 to 3
- out_weight: bfloat16 [4096, 4096], P('head', 'tm'), may hold values from -0.09375 to 0.09375
Outputs:
- layer_out: bfloat16 [8192, 4096], P('tm', 'head')
Inputs may be any that keep to these rules, and one draw needn't show every extreme that they name: `boundaries`: the bound of a block of text rows held by index t of tm lies in t * 128 + 1 to (t + 1) * 128, and the bounds never fall.
All inputs are finite; a program needn't handle non-finite values.
Results may differ from a plain program's by a relative error of at most 0.0052.
Values may be sent and summed in bfloat16 or wider, within the bound.
A program may use at most 192 MiB of HBM per device.

v0:
```python
import functools

import jax
import jax.numpy as jnp
from jax import lax
from jax.experimental import pallas as pl
from jax.experimental.pallas import tpu as pltpu
from jax.sharding import PartitionSpec as P

MESH = pl.DeviceIdType.MESH
F32 = jnp.float32
BF16 = jnp.bfloat16
HDIM = 128
NORM_ROWS = 16
NN = (((1,), (0,)), ((), ()))
NT = (((1,), (1,)), ((), ()))
TN = (((0,), (0,)), ((), ()))


def dot(a, b, dims):
    return lax.dot_general(a, b, dims, preferred_element_type=F32)


def elu_one(values):
    return jnp.where(values > 0, values + 1.0, jnp.exp(jnp.minimum(values, 0.0)))


def split(value):
    high = value.astype(BF16)
    return high, (value - high.astype(F32)).astype(BF16)


def wait_bytes(ref, sem):
    pltpu.make_async_copy(ref, ref, sem).wait()


def kernel(
    ny,
    nz,
    nx,
    gy,
    gz,
    bound_ref,
    gate_ref,
    vk_ref,
    vv_ref,
    q_ref,
    tk_ref,
    tv_ref,
    w_ref,
    out_ref,
    w_all,
    kin,
    vown,
    vin,
    qin,
    tkin,
    tvin,
    bin_,
    kf,
    qf,
    s_send,
    s_recv,
    s_own,
    n_send,
    n_recv,
    n_own,
    sbuf,
    abuf,
    rbuf,
    tbuf,
    tsend,
    base,
    pbuf,
    pfx,
    numer_l,
    denom_l,
    local_o,
    mixed,
    far_send,
    far_recv,
    dir_send,
    dir_recv,
    sum_own,
    sum_fwd,
    fwd_send,
    fwd_recv,
    dsend,
    fin,
    in_sem,
    s_sem,
    w_sem,
    c_send,
    c_recv,
    w1_send,
    w1_recv,
    w2_send,
    w2_recv,
    a_send,
    a_recv,
    t_send,
    t_recv,
    p_send,
    p_recv,
    g_send,
    g_recv,
    m_send,
    m_recv,
    x_send,
    x_recv,
    d_send,
    d_recv,
):
    tm = lax.axis_index("tm")
    x = lax.axis_index("head")
    c = lax.rem(tm, 2)
    chip = tm // 2
    z = lax.rem(chip, nz)
    y = chip // nz

    vlen, width = vk_ref.shape
    rows = q_ref.shape[0]
    half_w = width // 2
    heads = half_w // HDIM
    per_head = nz // heads
    srows = HDIM // per_head
    wc = w_ref.shape[0]
    wh = wc // 2
    my, mz = ny // gy, nz // gz
    py, pz = lax.rem(y, gy), lax.rem(z, gz)
    yc, zc = y // gy, z // gz
    own_class = py * gz + pz
    offsets = [(dy, dz) for dy in range(gy) for dz in range(gz)]
    offsets.sort(key=lambda o: (o[0] + o[1], o[1]))

    def dev(t, xx):
        return {"tm": t, "head": xx}

    def y_dev(yy):
        return dev((yy * nz + z) * 2 + c, x)

    def z_dev(zz):
        return dev((y * nz + zz) * 2 + c, x)

    def x_dev(xx):
        return dev(tm, xx)

    def group_dev(dy, dz, core):
        yy = yc * gy + lax.rem(py + dy, gy)
        zz = zc * gz + lax.rem(pz + dz, gz)
        return dev((yy * nz + zz) * 2 + core, x)

    def class_of(dy, dz):
        return lax.rem(py + dy, gy) * gz + lax.rem(pz + dz, gz)

    twin = dev(tm + 1 - 2 * c, x)

    def ahead(me, step, n):
        return lax.rem(me + step, n)

    def send(src, dst, send_sem, recv_sem, device):
        copy = pltpu.make_async_remote_copy(
            src, dst, send_sem, recv_sem, device_id=device, device_id_type=MESH
        )
        copy.start()
        return copy

    mine = pl.ds(pl.multiple_of(c * half_w, HDIM), half_w)
    other = pl.ds(pl.multiple_of((1 - c) * half_w, HDIM), half_w)
    inputs = ((vk_ref, kin), (vv_ref, vin), (q_ref, qin), (tk_ref, tkin), (tv_ref, tvin))
    loads = [
        pltpu.make_async_copy(vk_ref, kin, in_sem.at[0]),
        pltpu.make_async_copy(vv_ref, vown, in_sem.at[1]),
        pltpu.make_async_copy(vv_ref.at[:, mine], vin.at[c], in_sem.at[5]),
    ] + [
        pltpu.make_async_copy(src.at[:, mine], dst.at[c], in_sem.at[i + 2])
        for i, (src, dst) in enumerate(inputs[2:])
    ]
    for load in loads:
        load.start()
    own_w = pltpu.make_async_copy(w_ref, w_all.at[yc, zc], w_sem)
    own_w.start()

    def far_first(n):
        return sorted(range(1, n), key=lambda step: -min(step, n - step))

    barrier = pltpu.get_barrier_semaphore()

    def greet(device):
        pl.semaphore_signal(barrier, inc=1, device_id=device, device_id_type=MESH)

    for step in far_first(nz):
        greet(z_dev(ahead(z, step, nz)))
    for step in far_first(ny):
        greet(y_dev(ahead(y, step, ny)))
    x_steps = [1, nx - 1] if nx > 2 else list(range(1, nx))
    for step in x_steps:
        greet(x_dev(ahead(x, step, nx)))
    greeted = 1 + (nz - 1) + (ny - 1) + len(x_steps)
    for dy, dz in offsets[1:]:
        greet(group_dev(dy, dz, 1 - c))
        greeted += 1
        if dy and dz:
            greet(group_dev(dy, dz, c))
            greeted += 1
    greet(twin)
    bin_[c] = jnp.full((8, HDIM), bound_ref[0], jnp.int32)

    loads[0].wait()
    kin[...] = elu_one(kin[...].astype(F32)).astype(BF16)
    loads[1].wait()
    ones = jnp.ones((NORM_ROWS, vlen), BF16)
    norm_row = lax.broadcasted_iota(jnp.int32, (NORM_ROWS, HDIM), 0)

    def own_state(core):
        norms = jnp.zeros((NORM_ROWS, HDIM), F32)
        states = []
        for h in range(heads):
            cols = pl.ds(pl.multiple_of(core * half_w + h * HDIM, HDIM), HDIM)
            feat = kin[:, cols]
            states.append(dot(feat, vown[:, cols], TN))
            norms = jnp.where(norm_row == h, dot(ones, feat, NN), norms)
        return states, norms

    states, norms = own_state(1 - c)
    for h in range(heads):
        for k in range(per_head):
            s_send[h * per_head + k] = states[h][k * srows : (k + 1) * srows].astype(BF16)
    n_send[...] = norms.astype(BF16)
    states, norms = own_state(c)
    for h in range(heads):
        for k in range(per_head):
            s_own[h * per_head + k] = states[h][k * srows : (k + 1) * srows]
    n_own[...] = norms
    kf[c] = kin[:, mine]
    pl.semaphore_wait(barrier, greeted)

    state_copy = send(s_send, s_recv, s_sem.at[0], s_sem.at[1], twin)
    norm_copy = send(n_send, n_recv, s_sem.at[2], s_sem.at[3], twin)
    def y_class(k):
        return y_dev(k * gy + py)

    def z_class(k):
        return z_dev(k * gz + pz)

    for step in far_first(mz):
        send(w_ref.at[0:wh], w_all.at[yc, zc, 0:wh], w1_send.at[0], w1_recv.at[0], z_class(ahead(zc, step, mz)))
    for step in far_first(my):
        send(w_ref.at[wh:wc], w_all.at[yc, zc, wh:wc], w1_send.at[1], w1_recv.at[1], y_class(ahead(yc, step, my)))

    state_copy.wait_recv()
    norm_copy.wait_recv()
    norms = (n_own[...] + n_recv[...].astype(F32)).astype(BF16)
    for k in range(nz):
        sbuf[k, 0:srows] = (s_own[k] + s_recv[k].astype(F32)).astype(BF16)
        sbuf[k, srows : srows + NORM_ROWS] = norms
    for step in far_first(nz):
        to = ahead(z, step, nz)
        send(sbuf.at[to], abuf.at[z], a_send, a_recv, z_dev(to))
    abuf[z] = sbuf[z]

    swaps = [send(kin.at[:, other], kf.at[c], c_send.at[0], c_recv.at[0], twin)]
    swaps += [
        send(src.at[:, other], dst.at[c], c_send.at[i + 1], c_recv.at[i + 1], twin)
        for i, (src, dst) in enumerate(inputs[1:])
    ]
    swaps.append(send(bin_.at[c], bin_.at[c], c_send.at[5], c_recv.at[5], twin))

    def bundle(half, index, q):
        if half == 0:
            return w_all.at[index, q * (mz // 2) : (q + 1) * (mz // 2), 0:wh]
        return w_all.at[q * (my // 2) : (q + 1) * (my // 2), index, wh:wc]

    laps = {}
    waited = set()

    def arrived(key):
        if key in laps and key not in waited:
            waited.add(key)
            laps[key].wait_recv()

    def lap(s, q):
        for half in range(2):
            for way in range(2):
                n, me = (my, yc) if half == 0 else (mz, zc)
                if s >= n // 2 or (s == n // 2 - 1 and q != way):
                    continue
                arrived((half, way, s - 1, q))
                block = ahead(me, n - s, n) if way == 0 else ahead(me, s, n)
                to = ahead(me, 1, n) if way == 0 else ahead(me, n - 1, n)
                part = bundle(half, block, q)
                laps[(half, way, s, q)] = send(
                    part, part, w2_send.at[half, way, s, q], w2_recv.at[half, way, s, q],
                    y_class(to) if half == 0 else z_class(to),
                )

    for load in loads[2:]:
        load.wait()
    for swap in swaps:
        swap.wait_recv()
    bounds = jnp.concatenate(
        [jnp.broadcast_to(bin_[0, 0:1, :], (rows, HDIM)), jnp.broadcast_to(bin_[1, 0:1, :], (rows, HDIM))]
    )
    row_ids = lax.broadcasted_iota(jnp.int32, (2 * rows, HDIM), 0)
    col_ids = lax.broadcasted_iota(jnp.int32, (2 * rows, HDIM), 1)

    def own_part(h):
        cols = slice(h * HDIM, (h + 1) * HDIM)
        query = qin[:, :, cols].reshape(2 * rows, HDIM)
        q_feat = elu_one(query.astype(F32)).astype(BF16)
        qf[h] = q_feat
        numer = jnp.zeros((2 * rows, HDIM), F32)
        denom = jnp.zeros((2 * rows, 1), F32)
        for e in range(2):
            weight = dot(q_feat, kf[e, :, cols], NT)
            weight = jnp.where(col_ids + (chip * 2 + e) * vlen < bounds, weight, 0.0)
            high, low = split(weight)
            values = vin[e, :, cols]
            numer = numer + dot(high, values, NN) + dot(low, values, NN)
            denom = denom + jnp.sum(weight, axis=1, keepdims=True)
        numer_l[h] = numer
        denom_l[h] = jnp.broadcast_to(denom, (2 * rows, HDIM))
        scores = dot(query, tkin[:, :, cols].reshape(2 * rows, HDIM), NT) * (float(HDIM) ** -0.5)
        causal = jnp.logical_and(col_ids <= row_ids, col_ids // rows == row_ids // rows)
        scores = jnp.where(causal, scores, -jnp.inf)
        expo = jnp.exp(scores - jnp.max(scores, axis=1, keepdims=True))
        probs = (expo / jnp.sum(expo, axis=1, keepdims=True)).astype(BF16)
        local_o[h] = dot(probs, tvin[:, :, cols].reshape(2 * rows, HDIM), NN)

    own_part(0)

    wait_bytes(abuf.at[0 : nz - 1], a_recv)
    total = jnp.zeros((srows + NORM_ROWS, HDIM), F32)
    for k in range(nz):
        rbuf[k] = total
        total = total + abuf[k].astype(F32)
    tsend[...] = total.astype(BF16)
    for step in range(1, ny):

        @pl.when(y + step < ny)
        def _():
            send(tsend, tbuf.at[y], t_send.at[step], t_recv.at[y], y_dev(y + step))

    own_w.wait()
    if mz > 1:
        wait_bytes(w_all.at[0, 0 : mz - 1, 0:wh], w1_recv.at[0])
    if my > 1:
        wait_bytes(w_all.at[0 : my - 1, 0, wh:wc], w1_recv.at[1])
    steps = max(my, mz) // 2
    if steps:
        lap(0, 0)
        lap(0, 1)

    for h in range(1, max(1, heads - 1)):
        own_part(h)

    base[...] = jnp.zeros_like(base)
    for k in range(ny - 1):

        @pl.when(k < y)
        def _():
            wait_bytes(tbuf.at[k], t_recv.at[k])
            base[...] += tbuf[k].astype(F32)

    for k in range(nz):
        pbuf[k] = (base[0:srows] + rbuf[k, 0:srows]).astype(BF16)
    pfx[z] = pbuf[z]
    for step in far_first(nz):
        to = ahead(z, step, nz)
        send(pbuf.at[to], pfx.at[z], p_send, p_recv, z_dev(to))
    norm_high, norm_low = split(base[srows : srows + NORM_ROWS] + rbuf[z, srows : srows + NORM_ROWS])

    for h in range(max(1, heads - 1), heads):
        own_part(h)

    wait_bytes(pfx.at[0 : nz - 1], p_recv)
    for s in range(1, steps):
        lap(s, 0)
        lap(s, 1)

    def retrieve(h):
        query = qf[h]
        first = h * per_head
        state = pfx[first : first + per_head].reshape(HDIM, HDIM)
        numer = numer_l[h] + dot(query, state, NN)
        denom = (dot(query, norm_high, NT) + dot(query, norm_low, NT))[:, h : h + 1] + denom_l[h]
        gate = 1.0 / (1.0 + jnp.exp(-jnp.full((8, HDIM), gate_ref[c * heads + h], F32)))[0:1]
        value = gate * (numer / denom) + (1.0 - gate) * local_o[h]
        mixed[own_class, c * heads + h] = value.astype(BF16)

    split_n = 2 if heads > 1 else 1

    def mixed_part(cls, i):
        return mixed.at[cls, pl.ds(c * heads + i * (heads // split_n), heads // split_n)]

    group_copies, twin_copies = {}, {}
    for i in range(split_n):
        for h in range(i * heads // split_n, (i + 1) * heads // split_n):
            retrieve(h)
        part = mixed_part(own_class, i)
        for r, (dy, dz) in reversed(list(enumerate(offsets))):
            if r == 0:
                twin_copies[r, i] = send(part, part, m_send.at[r, i], m_recv.at[r, i], twin)
            else:
                group_copies[r, i] = send(part, part, g_send.at[r, i], g_recv.at[r, i], group_dev(dy, dz, c))
    state_copy.wait_send()
    norm_copy.wait_send()
    for copy in swaps:
        copy.wait_send()
    if mz > 1:
        wait_bytes(w_all.at[0, 0 : mz - 1, 0:wh], w1_send.at[0])
    if my > 1:
        wait_bytes(w_all.at[0 : my - 1, 0, wh:wc], w1_send.at[1])
    wait_bytes(sbuf.at[0 : nz - 1], a_send)
    for step in range(1, ny):

        @pl.when(y + step < ny)
        def _():
            wait_bytes(tsend, t_send.at[step])

    wait_bytes(pbuf.at[0 : nz - 1], p_send)
    for key in list(laps):
        arrived(key)
    for copy in laps.values():
        copy.wait_send()

    yx = my // nx

    def project(cls, xxs):
        both = jnp.concatenate([mixed[cls, h] for h in range(2 * heads)], axis=1)
        block = jnp.concatenate([w_all[pl.ds(xx * yx, yx)].reshape(yx * mz * wc, width) for xx in xxs])
        value = dot(both, block, NT)
        return [value[:, i * HDIM : (i + 1) * HDIM] for i in range(len(xxs))]

    far_copies, dir_copies, fwd_copies = [], [], []

    def forward(r):
        to = ahead(x, 1 if r % 2 == 0 else nx - 1, nx)
        far_copies[r].wait_recv()
        fwd_send[r] = (sum_fwd[r] + far_recv[r].astype(F32)).astype(BF16)
        fwd_copies.append(send(fwd_send.at[r], fwd_recv.at[r], x_send.at[r, 2], x_recv.at[r, 2], x_dev(to)))

    def hand_over(r):
        for i in range(split_n):
            group_copies[r, i].wait_recv()
            part = mixed_part(class_of(*offsets[r]), i)
            twin_copies[r, i] = send(part, part, m_send.at[r, i], m_recv.at[r, i], twin)

    for r, (dy, dz) in enumerate(offsets):
        cls = class_of(dy, dz)
        for i in range(split_n):
            twin_copies[r, i].wait_recv()
        if nx == 4:
            near, away = (1, 3) if r % 2 == 0 else (3, 1)
            far, direct = project(cls, [ahead(x, 2, nx), ahead(x, away, nx)])
            far_send[r] = far.astype(BF16)
            far_copies.append(
                send(far_send.at[r], far_recv.at[r], x_send.at[r, 0], x_recv.at[r, 0], x_dev(ahead(x, near, nx)))
            )
            dir_send[r] = direct.astype(BF16)
            dir_copies.append(
                send(dir_send.at[r], dir_recv.at[r], x_send.at[r, 1], x_recv.at[r, 1], x_dev(ahead(x, away, nx)))
            )
            sum_fwd[r], sum_own[r] = project(cls, [ahead(x, near, nx), x])
            if r > 0:
                forward(r - 1)
        elif nx == 2:
            direct, sum_own[r] = project(cls, [1 - x, x])
            dir_send[r] = direct.astype(BF16)
            dir_copies.append(
                send(dir_send.at[r], dir_recv.at[r], x_send.at[r, 1], x_recv.at[r, 1], x_dev(1 - x))
            )
        else:
            (sum_own[r],) = project(cls, [x])
        for later in {0: (1, 2), 1: (3,)}.get(r, ()):
            if later < len(offsets):
                hand_over(later)
    if nx == 4:
        forward(len(offsets) - 1)

    done_copies = []
    for r, (dy, dz) in enumerate(offsets):
        total = sum_own[r]
        for copies, landed in ((dir_copies, dir_recv), (fwd_copies, fwd_recv)):
            if copies:
                copies[r].wait_recv()
                total = total + landed[r].astype(F32)
        total = total.astype(BF16)
        for e in range(2):
            dsend[r, e] = total[e * rows : (e + 1) * rows]
        place = fin.at[own_class * 2 + c]
        if r == 0:
            fin[own_class * 2 + c] = dsend[0, c]
            done_copies.append(send(dsend.at[0, 1 - c], place, d_send, d_recv, twin))
        else:
            for e in range(2):
                done_copies.append(send(dsend.at[r, e], place, d_send, d_recv, group_dev(dy, dz, e)))
    wait_bytes(fin.at[0 : len(done_copies)], d_recv)

    lane = lax.broadcasted_iota(jnp.int32, (rows, HDIM), 1)
    runs = HDIM // wc
    for b in range(out_ref.shape[1] // HDIM):
        value = jnp.zeros((rows, HDIM), F32)
        for k in range(runs):
            shard, e = divmod(b * runs + k, 2)
            yl, zz = divmod(shard, nz)
            pos = ((yl // gy) * mz + zz // gz) * wc
            piece = fin[((yl % gy) * gz + zz % gz) * 2 + e].astype(F32)
            shift = (k * wc - pos) % HDIM
            if shift:
                piece = pltpu.roll(piece, shift, 1)
            value = jnp.where(lane // wc == k, piece, value)
        out_ref[:, b * HDIM : (b + 1) * HDIM] = value.astype(BF16)

    for copies in (twin_copies.values(), group_copies.values(), far_copies, dir_copies, fwd_copies):
        for copy in copies:
            copy.wait_send()
    wait_bytes(fin.at[0 : len(done_copies)], d_send)


def local(grid, vk, vv, q, tk, tv, bounds, gate, w):
    ny, nz, nx, gy, gz = grid
    vlen, width = vk.shape
    rows = q.shape[0]
    half_w = width // 2
    heads = half_w // HDIM
    srows = half_w // nz
    wt = w.T
    wc = wt.shape[0]
    my, mz = ny // gy, nz // gz
    n = gy * gz
    assert (my // nx) * mz * wc == HDIM
    steps = max(my, mz, 2) // 2
    hbm = pl.BlockSpec(memory_space=pltpu.HBM)
    smem = pl.BlockSpec(memory_space=pltpu.SMEM)
    dma = pltpu.SemaphoreType.DMA
    slices = (nz, srows + NORM_ROWS, HDIM)
    states = (nz, srows, HDIM)
    per_head = (heads, 2 * rows, HDIM)
    blocks = (n, 2 * rows, HDIM)
    return pl.pallas_call(
        functools.partial(kernel, ny, nz, nx, gy, gz),
        out_shape=jax.ShapeDtypeStruct((rows, 2 * n * HDIM), BF16),
        in_specs=[smem, smem] + [hbm] * 6,
        out_specs=pl.BlockSpec(memory_space=pltpu.VMEM),
        scratch_shapes=[
            pltpu.VMEM((my, mz, wc, width), BF16),
            pltpu.VMEM((vlen, width), BF16),
            pltpu.VMEM((vlen, width), BF16),
            pltpu.VMEM((2, vlen, half_w), BF16),
            pltpu.VMEM((2, rows, half_w), BF16),
            pltpu.VMEM((2, rows, half_w), BF16),
            pltpu.VMEM((2, rows, half_w), BF16),
            pltpu.VMEM((2, 8, HDIM), jnp.int32),
            pltpu.VMEM((2, vlen, half_w), BF16),
            pltpu.VMEM(per_head, BF16),
            pltpu.VMEM(states, BF16),
            pltpu.VMEM(states, BF16),
            pltpu.VMEM(states, F32),
            pltpu.VMEM((NORM_ROWS, HDIM), BF16),
            pltpu.VMEM((NORM_ROWS, HDIM), BF16),
            pltpu.VMEM((NORM_ROWS, HDIM), F32),
            pltpu.VMEM(slices, BF16),
            pltpu.VMEM(slices, BF16),
            pltpu.VMEM(slices, F32),
            pltpu.VMEM((ny, srows + NORM_ROWS, HDIM), BF16),
            pltpu.VMEM((srows + NORM_ROWS, HDIM), BF16),
            pltpu.VMEM((srows + NORM_ROWS, HDIM), F32),
            pltpu.VMEM(states, BF16),
            pltpu.VMEM(states, BF16),
            pltpu.VMEM(per_head, F32),
            pltpu.VMEM(per_head, F32),
            pltpu.VMEM(per_head, F32),
            pltpu.VMEM((n, 2 * heads, 2 * rows, HDIM), BF16),
            pltpu.VMEM(blocks, BF16),
            pltpu.VMEM(blocks, BF16),
            pltpu.VMEM(blocks, BF16),
            pltpu.VMEM(blocks, BF16),
            pltpu.VMEM(blocks, F32),
            pltpu.VMEM(blocks, F32),
            pltpu.VMEM(blocks, BF16),
            pltpu.VMEM(blocks, BF16),
            pltpu.VMEM((n, 2, rows, HDIM), BF16),
            pltpu.VMEM((2 * n, rows, HDIM), BF16),
            dma((6,)),
            dma((4,)),
            dma,
            dma((6,)),
            dma((6,)),
            dma((2,)),
            dma((2,)),
            dma((2, 2, steps, 2)),
            dma((2, 2, steps, 2)),
            dma,
            dma,
            dma((ny,)),
            dma((ny,)),
            dma,
            dma,
            dma((n, 2)),
            dma((n, 2)),
            dma((n, 2)),
            dma((n, 2)),
            dma((n, 3)),
            dma((n, 3)),
            dma,
            dma,
        ],
        compiler_params=pltpu.CompilerParams(
            collective_id=0, has_side_effects=True, vmem_limit_bytes=60 * 1024 * 1024
        ),
    )(bounds, gate, vk, vv, q, tk, tv, wt)


def solution(mesh):
    nx = mesh.shape["head"]
    specs = (
        P("tm", "head"),
        P("tm", "head"),
        P("tm", "head"),
        P("tm", "head"),
        P("tm", "head"),
        P("tm"),
        P("head"),
        P("head", "tm"),
    )
    return jax.shard_map(
        functools.partial(local, (8, mesh.shape["tm"] // 16, nx, 2, 2)),
        mesh=mesh,
        in_specs=specs,
        out_specs=P("tm", "head"),
        check_vma=False,
    )
```

profile of v0, /device:TPU:1, one launch (start us, length us, event | category | flops | bytes accessed | tf_op | source)
XLA Modules:
  0.0 62.3 jit_solution(4948240409348043580)
XLA Ops:
  0.7 60.1 %shard_map.82 = bf16[64,1024]{1,0:T(8,128)(2,1)} custom-call(s32[1]{0:T(128)S(6)} %copy.10.bound_ref, f32[8]{0:T(128)} %gate_ref.1, bf16[128,1024]{1,0:T(8,128)(2,1)} %vk_ref.1, bf16[128,1024]{1,0:T(8,128)(2,1)} %vv_ref.1, bf16[64,1024]{1,0:T(8,128)(2,1)} %q_ref.1, bf16[64,1024]{1,0:T(8,128)(2,1)} %tk_ref.1, bf16[64,1024]{1,0:T(8,128)(2,1)} %tv_ref.1, ...), custom_call_target="tpu_custom_call" | custom-call | tf_op jit(solution)/shard_map/pallas_call | solution.py:541
  60.7 1.6 %copy.11 = bf16[64,1024]{1,0:T(8,128)(2,1)} copy(bf16[64,1024]{1,0:T(8,128)(2,1)} %shard_map.82) | data formatting | bytes 262144
where the time goes:
time: 62.5 us; the launch traced here: 62.3 us
  Pallas kernels  60.1 us (96%)
  local copies, waits for them, and re-layouts  1.57 us (3%)
  between operations  0.66 us (1%)
    pallas_call x1, Pallas kernels, local(): pl.pallas_call(functools.partial(kernel, ny, nz, nx, gy, gz), out_shape=j...  60.1 us
    unnamed x1, local copies, waits for them, and re-layouts  1.57 us

commit v1 on v0

--- a/solution.py
+++ b/solution.py
@@ -77,14 +77,9 @@
     denom_l,
     local_o,
     mixed,
-    far_send,
-    far_recv,
-    dir_send,
-    dir_recv,
+    x_out,
+    x_in,
     sum_own,
-    sum_fwd,
-    fwd_send,
-    fwd_recv,
     dsend,
     fin,
     in_sem,
@@ -193,10 +188,10 @@
         greet(z_dev(ahead(z, step, nz)))
     for step in far_first(ny):
         greet(y_dev(ahead(y, step, ny)))
-    x_steps = [1, nx - 1] if nx > 2 else list(range(1, nx))
-    for step in x_steps:
+    x_order = far_first(nx) + [0]
+    for step in x_order[:-1]:
         greet(x_dev(ahead(x, step, nx)))
-    greeted = 1 + (nz - 1) + (ny - 1) + len(x_steps)
+    greeted = 1 + (nz - 1) + (ny - 1) + (nx - 1)
     for dy, dz in offsets[1:]:
         greet(group_dev(dy, dz, 1 - c))
         greeted += 1
@@ -329,18 +324,6 @@
 
     own_part(0)
 
-    wait_bytes(abuf.at[0 : nz - 1], a_recv)
-    total = jnp.zeros((srows + NORM_ROWS, HDIM), F32)
-    for k in range(nz):
-        rbuf[k] = total
-        total = total + abuf[k].astype(F32)
-    tsend[...] = total.astype(BF16)
-    for step in range(1, ny):
-
-        @pl.when(y + step < ny)
-        def _():
-            send(tsend, tbuf.at[y], t_send.at[step], t_recv.at[y], y_dev(y + step))
-
     own_w.wait()
     if mz > 1:
         wait_bytes(w_all.at[0, 0 : mz - 1, 0:wh], w1_recv.at[0])
@@ -351,6 +334,18 @@
         lap(0, 0)
         lap(0, 1)
 
+    wait_bytes(abuf.at[0 : nz - 1], a_recv)
+    total = jnp.zeros((srows + NORM_ROWS, HDIM), F32)
+    for k in range(nz):
+        rbuf[k] = total
+        total = total + abuf[k].astype(F32)
+    tsend[...] = total.astype(BF16)
+    for step in range(1, ny):
+
+        @pl.when(y + step < ny)
+        def _():
+            send(tsend, tbuf.at[y], t_send.at[step], t_recv.at[y], y_dev(y + step))
+
     for h in range(1, max(1, heads - 1)):
         own_part(h)
 
@@ -373,10 +368,11 @@
     for h in range(max(1, heads - 1), heads):
         own_part(h)
 
-    wait_bytes(pfx.at[0 : nz - 1], p_recv)
     for s in range(1, steps):
         lap(s, 0)
         lap(s, 1)
+
+    wait_bytes(pfx.at[0 : nz - 1], p_recv)
 
     def retrieve(h):
         query = qf[h]
@@ -432,59 +428,38 @@
         value = dot(both, block, NT)
         return [value[:, i * HDIM : (i + 1) * HDIM] for i in range(len(xxs))]
 
-    far_copies, dir_copies, fwd_copies = [], [], []
-
-    def forward(r):
-        to = ahead(x, 1 if r % 2 == 0 else nx - 1, nx)
-        far_copies[r].wait_recv()
-        fwd_send[r] = (sum_fwd[r] + far_recv[r].astype(F32)).astype(BF16)
-        fwd_copies.append(send(fwd_send.at[r], fwd_recv.at[r], x_send.at[r, 2], x_recv.at[r, 2], x_dev(to)))
+    x_copies = {}
 
     def hand_over(r):
         for i in range(split_n):
+            part = mixed_part(class_of(*offsets[r]), i)
             group_copies[r, i].wait_recv()
-            part = mixed_part(class_of(*offsets[r]), i)
             twin_copies[r, i] = send(part, part, m_send.at[r, i], m_recv.at[r, i], twin)
 
     for r, (dy, dz) in enumerate(offsets):
         cls = class_of(dy, dz)
         for i in range(split_n):
             twin_copies[r, i].wait_recv()
-        if nx == 4:
-            near, away = (1, 3) if r % 2 == 0 else (3, 1)
-            far, direct = project(cls, [ahead(x, 2, nx), ahead(x, away, nx)])
-            far_send[r] = far.astype(BF16)
-            far_copies.append(
-                send(far_send.at[r], far_recv.at[r], x_send.at[r, 0], x_recv.at[r, 0], x_dev(ahead(x, near, nx)))
-            )
-            dir_send[r] = direct.astype(BF16)
-            dir_copies.append(
-                send(dir_send.at[r], dir_recv.at[r], x_send.at[r, 1], x_recv.at[r, 1], x_dev(ahead(x, away, nx)))
-            )
-            sum_fwd[r], sum_own[r] = project(cls, [ahead(x, near, nx), x])
-            if r > 0:
-                forward(r - 1)
-        elif nx == 2:
-            direct, sum_own[r] = project(cls, [1 - x, x])
-            dir_send[r] = direct.astype(BF16)
-            dir_copies.append(
-                send(dir_send.at[r], dir_recv.at[r], x_send.at[r, 1], x_recv.at[r, 1], x_dev(1 - x))
-            )
-        else:
-            (sum_own[r],) = project(cls, [x])
+        for first in range(0, len(x_order), 2):
+            part_steps = x_order[first : first + 2]
+            for step, value in zip(part_steps, project(cls, [ahead(x, step, nx) for step in part_steps])):
+                if step == 0:
+                    sum_own[r] = value
+                    continue
+                x_out[r, step] = value.astype(BF16)
+                x_copies[r, step] = send(
+                    x_out.at[r, step], x_in.at[r, step], x_send.at[r, step], x_recv.at[r, step],
+                    x_dev(ahead(x, step, nx)),
+                )
         for later in {0: (1, 2), 1: (3,)}.get(r, ()):
             if later < len(offsets):
                 hand_over(later)
-    if nx == 4:
-        forward(len(offsets) - 1)
-
     done_copies = []
     for r, (dy, dz) in enumerate(offsets):
         total = sum_own[r]
-        for copies, landed in ((dir_copies, dir_recv), (fwd_copies, fwd_recv)):
-            if copies:
-                copies[r].wait_recv()
-                total = total + landed[r].astype(F32)
+        for step in x_order[:-1]:
+            x_copies[r, step].wait_recv()
+            total = total + x_in[r, step].astype(F32)
         total = total.astype(BF16)
         for e in range(2):
             dsend[r, e] = total[e * rows : (e + 1) * rows]
@@ -512,7 +487,7 @@
             value = jnp.where(lane // wc == k, piece, value)
         out_ref[:, b * HDIM : (b + 1) * HDIM] = value.astype(BF16)
 
-    for copies in (twin_copies.values(), group_copies.values(), far_copies, dir_copies, fwd_copies):
+    for copies in (twin_copies.values(), group_copies.values(), x_copies.values()):
         for copy in copies:
             copy.wait_send()
     wait_bytes(fin.at[0 : len(done_copies)], d_send)
@@ -537,7 +512,6 @@
     slices = (nz, srows + NORM_ROWS, HDIM)
     states = (nz, srows, HDIM)
     per_head = (heads, 2 * rows, HDIM)
-    blocks = (n, 2 * rows, HDIM)
     return pl.pallas_call(
         functools.partial(kernel, ny, nz, nx, gy, gz),
         out_shape=jax.ShapeDtypeStruct((rows, 2 * n * HDIM), BF16),
@@ -572,14 +546,9 @@
             pltpu.VMEM(per_head, F32),
             pltpu.VMEM(per_head, F32),
             pltpu.VMEM((n, 2 * heads, 2 * rows, HDIM), BF16),
-            pltpu.VMEM(blocks, BF16),
-            pltpu.VMEM(blocks, BF16),
-            pltpu.VMEM(blocks, BF16),
-            pltpu.VMEM(blocks, BF16),
-            pltpu.VMEM(blocks, F32),
-            pltpu.VMEM(blocks, F32),
-            pltpu.VMEM(blocks, BF16),
-            pltpu.VMEM(blocks, BF16),
+            pltpu.VMEM((n, nx, 2 * rows, HDIM), BF16),
+            pltpu.VMEM((n, nx, 2 * rows, HDIM), BF16),
+            pltpu.VMEM((n, 2 * rows, HDIM), F32),
             pltpu.VMEM((n, 2, rows, HDIM), BF16),
             pltpu.VMEM((2 * n, rows, HDIM), BF16),
             dma((6,)),
@@ -601,8 +570,8 @@
             dma((n, 2)),
             dma((n, 2)),
             dma((n, 2)),
-            dma((n, 3)),
-            dma((n, 3)),
+            dma((n, nx)),
+            dma((n, nx)),
             dma,
             dma,
         ],

time: 62.5 us -> 61.2 us (0.979)
  the two profiles are of different devices: /device:TPU:1 before, /device:TPU:49 now
where the time goes in v1:
time: 61.2 us; the launch traced here: 61 us
  Pallas kernels  58.8 us (96%)
  local copies, waits for them, and re-layouts  1.57 us (3%)
  between operations  0.66 us (1%)
    pallas_call x1, Pallas kernels, local(): pl.pallas_call(functools.partial(kernel, ny, nz, nx, gy, gz), out_shape=j...  58.8 us
    unnamed x1, local copies, waits for them, and re-layouts  1.57 us

profile of v1, /device:TPU:49, one launch (start us, length us, event | category | flops | bytes accessed | tf_op | source)
XLA Modules:
  0.0 61.0 jit_solution(4305121669839442257)
XLA Ops:
  0.7 58.8 %shard_map.82 = bf16[64,1024]{1,0:T(8,128)(2,1)} custom-call(s32[1]{0:T(128)S(6)} %copy.10.bound_ref, f32[8]{0:T(128)} %gate_ref.1, bf16[128,1024]{1,0:T(8,128)(2,1)} %vk_ref.1, bf16[128,1024]{1,0:T(8,128)(2,1)} %vv_ref.1, bf16[64,1024]{1,0:T(8,128)(2,1)} %q_ref.1, bf16[64,1024]{1,0:T(8,128)(2,1)} %tk_ref.1, bf16[64,1024]{1,0:T(8,128)(2,1)} %tv_ref.1, ...), custom_call_target="tpu_custom_call" | custom-call | tf_op jit(solution)/shard_map/pallas_call | solution.py:515
  59.5 1.6 %copy.11 = bf16[64,1024]{1,0:T(8,128)(2,1)} copy(bf16[64,1024]{1,0:T(8,128)(2,1)} %shard_map.82) | data formatting | bytes 262144

commit v2 on v1

--- a/solution.py
+++ b/solution.py
@@ -70,7 +70,6 @@
     rbuf,
     tbuf,
     tsend,
-    base,
     pbuf,
     pfx,
     numer_l,
@@ -164,9 +163,10 @@
     other = pl.ds(pl.multiple_of((1 - c) * half_w, HDIM), half_w)
     inputs = ((vk_ref, kin), (vv_ref, vin), (q_ref, qin), (tk_ref, tkin), (tv_ref, tvin))
     loads = [
-        pltpu.make_async_copy(vk_ref, kin, in_sem.at[0]),
-        pltpu.make_async_copy(vv_ref, vown, in_sem.at[1]),
-        pltpu.make_async_copy(vv_ref.at[:, mine], vin.at[c], in_sem.at[5]),
+        pltpu.make_async_copy(vk_ref.at[:, other], kin.at[0], in_sem.at[0]),
+        pltpu.make_async_copy(vv_ref.at[:, other], vown, in_sem.at[1]),
+        pltpu.make_async_copy(vk_ref.at[:, mine], kin.at[1], in_sem.at[5]),
+        pltpu.make_async_copy(vv_ref.at[:, mine], vin.at[c], in_sem.at[6]),
     ] + [
         pltpu.make_async_copy(src.at[:, mine], dst.at[c], in_sem.at[i + 2])
         for i, (src, dst) in enumerate(inputs[2:])
@@ -202,47 +202,53 @@
     bin_[c] = jnp.full((8, HDIM), bound_ref[0], jnp.int32)
 
     loads[0].wait()
-    kin[...] = elu_one(kin[...].astype(F32)).astype(BF16)
+    kin[0] = elu_one(kin[0].astype(F32)).astype(BF16)
     loads[1].wait()
     ones = jnp.ones((NORM_ROWS, vlen), BF16)
     norm_row = lax.broadcasted_iota(jnp.int32, (NORM_ROWS, HDIM), 0)
 
-    def own_state(core):
+    def own_state(keys, values):
         norms = jnp.zeros((NORM_ROWS, HDIM), F32)
         states = []
         for h in range(heads):
-            cols = pl.ds(pl.multiple_of(core * half_w + h * HDIM, HDIM), HDIM)
-            feat = kin[:, cols]
-            states.append(dot(feat, vown[:, cols], TN))
-            norms = jnp.where(norm_row == h, dot(ones, feat, NN), norms)
+            cols = slice(h * HDIM, (h + 1) * HDIM)
+            states.append(dot(keys[:, cols], values[:, cols], TN))
+            norms = jnp.where(norm_row == h, dot(ones, keys[:, cols], NN), norms)
         return states, norms
 
-    states, norms = own_state(1 - c)
+    states, norms = own_state(kin.at[0], vown)
     for h in range(heads):
         for k in range(per_head):
             s_send[h * per_head + k] = states[h][k * srows : (k + 1) * srows].astype(BF16)
     n_send[...] = norms.astype(BF16)
-    states, norms = own_state(c)
+    for k in range(ny):
+
+        @pl.when(k >= y)
+        def _():
+            tbuf[k] = jnp.zeros(tbuf.shape[1:], BF16)
+
+    pl.semaphore_wait(barrier, greeted)
+    state_copy = send(s_send, s_recv, s_sem.at[0], s_sem.at[1], twin)
+    norm_copy = send(n_send, n_recv, s_sem.at[2], s_sem.at[3], twin)
+    def y_class(k):
+        return y_dev(k * gy + py)
+
+    def z_class(k):
+        return z_dev(k * gz + pz)
+
+    for step in far_first(mz):
+        send(w_ref.at[0:wh], w_all.at[yc, zc, 0:wh], w1_send.at[0], w1_recv.at[0], z_class(ahead(zc, step, mz)))
+    for step in far_first(my):
+        send(w_ref.at[wh:wc], w_all.at[yc, zc, wh:wc], w1_send.at[1], w1_recv.at[1], y_class(ahead(yc, step, my)))
+
+    loads[2].wait()
+    kf[c] = elu_one(kin[1].astype(F32)).astype(BF16)
+    loads[3].wait()
+    states, norms = own_state(kf.at[c], vin.at[c])
     for h in range(heads):
         for k in range(per_head):
             s_own[h * per_head + k] = states[h][k * srows : (k + 1) * srows]
     n_own[...] = norms
-    kf[c] = kin[:, mine]
-    pl.semaphore_wait(barrier, greeted)
-
-    state_copy = send(s_send, s_recv, s_sem.at[0], s_sem.at[1], twin)
-    norm_copy = send(n_send, n_recv, s_sem.at[2], s_sem.at[3], twin)
-    def y_class(k):
-        return y_dev(k * gy + py)
-
-    def z_class(k):
-        return z_dev(k * gz + pz)
-
-    for step in far_first(mz):
-        send(w_ref.at[0:wh], w_all.at[yc, zc, 0:wh], w1_send.at[0], w1_recv.at[0], z_class(ahead(zc, step, mz)))
-    for step in far_first(my):
-        send(w_ref.at[wh:wc], w_all.at[yc, zc, wh:wc], w1_send.at[1], w1_recv.at[1], y_class(ahead(yc, step, my)))
-
     state_copy.wait_recv()
     norm_copy.wait_recv()
     norms = (n_own[...] + n_recv[...].astype(F32)).astype(BF16)
@@ -254,7 +260,7 @@
         send(sbuf.at[to], abuf.at[z], a_send, a_recv, z_dev(to))
     abuf[z] = sbuf[z]
 
-    swaps = [send(kin.at[:, other], kf.at[c], c_send.at[0], c_recv.at[0], twin)]
+    swaps = [send(kin.at[0], kf.at[c], c_send.at[0], c_recv.at[0], twin)]
     swaps += [
         send(src.at[:, other], dst.at[c], c_send.at[i + 1], c_recv.at[i + 1], twin)
         for i, (src, dst) in enumerate(inputs[1:])
@@ -274,8 +280,8 @@
             waited.add(key)
             laps[key].wait_recv()
 
-    def lap(s, q):
-        for half in range(2):
+    def lap(s, q, halves=(0, 1)):
+        for half in halves:
             for way in range(2):
                 n, me = (my, yc) if half == 0 else (mz, zc)
                 if s >= n // 2 or (s == n // 2 - 1 and q != way):
@@ -289,7 +295,7 @@
                     y_class(to) if half == 0 else z_class(to),
                 )
 
-    for load in loads[2:]:
+    for load in loads[4:]:
         load.wait()
     for swap in swaps:
         swap.wait_recv()
@@ -322,17 +328,12 @@
         probs = (expo / jnp.sum(expo, axis=1, keepdims=True)).astype(BF16)
         local_o[h] = dot(probs, tvin[:, :, cols].reshape(2 * rows, HDIM), NN)
 
-    own_part(0)
-
+    steps = max(my, mz) // 2
     own_w.wait()
-    if mz > 1:
-        wait_bytes(w_all.at[0, 0 : mz - 1, 0:wh], w1_recv.at[0])
     if my > 1:
         wait_bytes(w_all.at[0 : my - 1, 0, wh:wc], w1_recv.at[1])
-    steps = max(my, mz) // 2
-    if steps:
-        lap(0, 0)
-        lap(0, 1)
+        lap(0, 0, (1,))
+        lap(0, 1, (1,))
 
     wait_bytes(abuf.at[0 : nz - 1], a_recv)
     total = jnp.zeros((srows + NORM_ROWS, HDIM), F32)
@@ -340,23 +341,29 @@
         rbuf[k] = total
         total = total + abuf[k].astype(F32)
     tsend[...] = total.astype(BF16)
-    for step in range(1, ny):
+    for step in far_first(ny):
 
         @pl.when(y + step < ny)
         def _():
             send(tsend, tbuf.at[y], t_send.at[step], t_recv.at[y], y_dev(y + step))
 
-    for h in range(1, max(1, heads - 1)):
+    if mz > 1:
+        wait_bytes(w_all.at[0, 0 : mz - 1, 0:wh], w1_recv.at[0])
+        lap(0, 0, (0,))
+        lap(0, 1, (0,))
+
+    for h in range(heads // 2):
         own_part(h)
 
-    base[...] = jnp.zeros_like(base)
     for k in range(ny - 1):
 
         @pl.when(k < y)
         def _():
             wait_bytes(tbuf.at[k], t_recv.at[k])
-            base[...] += tbuf[k].astype(F32)
-
+
+    base = tbuf[0].astype(F32)
+    for k in range(1, ny):
+        base = base + tbuf[k].astype(F32)
     for k in range(nz):
         pbuf[k] = (base[0:srows] + rbuf[k, 0:srows]).astype(BF16)
     pfx[z] = pbuf[z]
@@ -365,7 +372,7 @@
         send(pbuf.at[to], pfx.at[z], p_send, p_recv, z_dev(to))
     norm_high, norm_low = split(base[srows : srows + NORM_ROWS] + rbuf[z, srows : srows + NORM_ROWS])
 
-    for h in range(max(1, heads - 1), heads):
+    for h in range(heads // 2, heads):
         own_part(h)
 
     for s in range(1, steps):
@@ -519,8 +526,8 @@
         out_specs=pl.BlockSpec(memory_space=pltpu.VMEM),
         scratch_shapes=[
             pltpu.VMEM((my, mz, wc, width), BF16),
-            pltpu.VMEM((vlen, width), BF16),
-            pltpu.VMEM((vlen, width), BF16),
+            pltpu.VMEM((2, vlen, half_w), BF16),
+            pltpu.VMEM((vlen, half_w), BF16),
             pltpu.VMEM((2, vlen, half_w), BF16),
             pltpu.VMEM((2, rows, half_w), BF16),
             pltpu.VMEM((2, rows, half_w), BF16),
@@ -539,7 +546,6 @@
             pltpu.VMEM(slices, F32),
             pltpu.VMEM((ny, srows + NORM_ROWS, HDIM), BF16),
             pltpu.VMEM((srows + NORM_ROWS, HDIM), BF16),
-            pltpu.VMEM((srows + NORM_ROWS, HDIM), F32),
             pltpu.VMEM(states, BF16),
             pltpu.VMEM(states, BF16),
             pltpu.VMEM(per_head, F32),
@@ -551,7 +557,7 @@
             pltpu.VMEM((n, 2 * rows, HDIM), F32),
             pltpu.VMEM((n, 2, rows, HDIM), BF16),
             pltpu.VMEM((2 * n, rows, HDIM), BF16),
-            dma((6,)),
+            dma((7,)),
             dma((4,)),
             dma,
             dma((6,)),

time: 61.2 us -> 59.6 us (0.974)
  the two profiles are of different devices: /device:TPU:49 before, /device:TPU:1 now
where the time goes in v2:
time: 59.6 us; the launch traced here: 58.9 us
  Pallas kernels  56.6 us (95%)
  local copies, waits for them, and re-layouts  1.57 us (3%)
  between operations  0.66 us (1%)
    pallas_call x1, Pallas kernels, local(): pl.pallas_call(functools.partial(kernel, ny, nz, nx, gy, gz), out_shape=j...  56.6 us
    unnamed x1, local copies, waits for them, and re-layouts  1.57 us

profile of v2, /device:TPU:1, one launch (start us, length us, event | category | flops | bytes accessed | tf_op | source)
XLA Modules:
  0.0 58.9 jit_solution(14035096506550384778)
XLA Ops:
  0.7 56.6 %shard_map.82 = bf16[64,1024]{1,0:T(8,128)(2,1)} custom-call(s32[1]{0:T(128)S(6)} %copy.10.bound_ref, f32[8]{0:T(128)} %gate_ref.1, bf16[128,1024]{1,0:T(8,128)(2,1)} %vk_ref.1, bf16[128,1024]{1,0:T(8,128)(2,1)} %vv_ref.1, bf16[64,1024]{1,0:T(8,128)(2,1)} %q_ref.1, bf16[64,1024]{1,0:T(8,128)(2,1)} %tk_ref.1, bf16[64,1024]{1,0:T(8,128)(2,1)} %tv_ref.1, ...), custom_call_target="tpu_custom_call" | custom-call | tf_op jit(solution)/shard_map/pallas_call | solution.py:522
  57.3 1.6 %copy.11 = bf16[64,1024]{1,0:T(8,128)(2,1)} copy(bf16[64,1024]{1,0:T(8,128)(2,1)} %shard_map.82) | data formatting | bytes 262144
